TPU v7x, 256 devices: a whole 4x4x8 slice. The times are simulated.
256 devices in a mesh: node: 64 (over x_hi, z, y), head: 4 (over x_lo, core).
Axes of the slice: x: 4 (x_hi: 2, x_lo: 2; x = x_hi * 2 + x_lo), y: 4, z: 8, core: 2. Of those that a mesh axis runs over, the one named last changes fastest.
Arguments:
- queries: bfloat16 [16384, 8192], P('node', 'head'), may hold values from -15 to 15
- own_cache: bfloat16 [2, 16384, 1024], P(None, 'node', 'head'), may hold values from -12 to 12
- tree_cache: bfloat16 [2, 65536, 1024], P(None, 'node', 'head'), may hold values from -6 to 6
- shared_cache: bfloat16 [2, 512, 1024], P(None, None, 'head'), may hold values from -6 to 6
- parent: int32 [128], replicated, may hold values from -1 to 127, as said below
- leaf: int32 [128], P('node'), may hold values from 0 to 127, as said below
Outputs:
- attended: bfloat16 [16384, 8192], P(('node', 'head'))
Inputs may be any that keep to these rules, and one draw needn't show every extreme that they name: The 128 tree blocks fall into runs of 8 consecutive blocks, counted cyclically (block 127 is followed by block 0); each run is one subtree: its first block has parent -1 and every other block's parent is an earlier block of the same run. Every path thus holds at most 8 blocks. Branch b hangs under a block of its own node: leaf[b] // 2 == b // 2, where block i lies on node i // 2. Every block on the path of a branch of node n lies on one of the nodes n - 4 to n, counted modulo 128 / 2. Some branch's path holds exactly 8 blocks and reaches node n - 4.
All inputs are finite; a program needn't handle non-finite values.
Results may differ from a plain program's by a relative error of at most 0.011.
Values may be sent and summed in bfloat16 or wider, within the bound.
A program may use at most 128 MiB of HBM per device.

v0:
```python
import math

import jax
import jax.numpy as jnp
from jax import lax
from jax.sharding import PartitionSpec as P

HD = 128
BT = 512
BQ = 128
SUB = 8
BLK_DEV = 2
REACH = 4


BASE = 1000000.0
NEG = -1e30


def from_behind(value, axis, steps):
    count = lax.axis_size(axis)
    pairs = [(source, (source + steps) % count) for source in range(count)]
    return lax.ppermute(value, axis, pairs)


def rotate(field, where_at):
    half = HD // 2
    inverse = jnp.power(jnp.float32(BASE), -jnp.arange(half).astype(jnp.float32) * (2.0 / HD))
    angle = where_at.astype(jnp.float32)[:, None] * inverse[None, :]
    cosine = jnp.cos(angle)[:, None, :]
    sine = jnp.sin(angle)[:, None, :]
    first = field[..., :half]
    second = field[..., half:]
    return jnp.concatenate(
        [first * cosine - second * sine, second * cosine + first * sine], axis=-1
    )


def path_of(leaf_ids, parent):
    chain = []
    current = leaf_ids
    for step in range(SUB):
        chain.append(current)
        current = jnp.where(current >= 0, parent[jnp.maximum(current, 0)], -1)
    return jnp.stack(chain, axis=-1)


def block_terms(query_block, keys, values, valid, mask):
    count = keys.shape[0]
    key_heads = keys.reshape(count, -1, HD)
    value_heads = values.reshape(count, -1, HD)
    scores = jnp.einsum(
        "qhgd,nhd->hgqn", query_block, key_heads, preferred_element_type=jnp.float32
    )
    scores = scores * (1.0 / math.sqrt(HD))
    if mask is not None:
        scores = jnp.where(mask, scores, NEG)
    peak = jnp.max(scores, axis=-1, keepdims=True)
    weights = jnp.exp(scores - peak)
    total = jnp.sum(weights, axis=-1)
    mixed = jnp.einsum(
        "hgqn,nhd->qhgd",
        weights.astype(jnp.bfloat16),
        value_heads,
        preferred_element_type=jnp.float32,
    )
    peak = jnp.transpose(peak[..., 0], (2, 0, 1))
    total = jnp.transpose(total, (2, 0, 1))
    peak = jnp.where(valid, peak, NEG)
    total = jnp.where(valid, total, 0.0)
    mixed = jnp.where(valid, mixed, 0.0)
    return (peak, total, mixed)


def combine(first, second):
    peak = jnp.maximum(first[0], second[0])
    left = jnp.exp(first[0] - peak)
    right = jnp.exp(second[0] - peak)
    return (
        peak,
        first[1] * left + second[1] * right,
        first[2] * left[..., None] + second[2] * right[..., None],
    )


def per_device(queries, own_cache, tree_cache, shared_cache, parent, leaf):
    nodes = lax.axis_size("node")
    here = lax.axis_index("node")
    branches = leaf.shape[0]
    heads = queries.shape[1] // HD
    key_heads = tree_cache.shape[2] // HD
    group = heads // key_heads
    rows = branches * BQ
    block_ids = path_of(leaf, parent)
    valid = block_ids >= 0
    depth = jnp.sum(valid.astype(jnp.int32), axis=1)
    offsets = jnp.arange(BQ, dtype=jnp.int32)
    positions = ((BT * (depth + 1))[:, None] + offsets[None, :]).reshape(rows)
    turned = rotate(queries.reshape(rows, heads, HD).astype(jnp.float32), positions).astype(
        jnp.bfloat16
    )
    turned = turned.reshape(rows, heads * HD)
    own_keys = rotate(own_cache[0].reshape(rows, key_heads, HD).astype(jnp.float32), positions)
    own_keys = own_keys.astype(jnp.bfloat16).reshape(rows, key_heads * HD)
    causal = offsets[:, None] >= offsets[None, :]
    states = []
    for branch in range(branches):
        first_row = branch * BQ
        query_block = turned[first_row : first_row + BQ].reshape(BQ, key_heads, group, HD)
        state = block_terms(query_block, shared_cache[0], shared_cache[1], True, None)
        state = combine(
            state,
            block_terms(
                query_block,
                own_keys[first_row : first_row + BQ],
                own_cache[1, first_row : first_row + BQ],
                True,
                causal,
            ),
        )
        states.append(state)
    pieces = [tree_cache]
    moving = tree_cache
    for hop in range(REACH):
        moving = from_behind(moving, "node", 1)
        pieces.append(moving)
    window = jnp.concatenate(pieces, axis=1)
    clamped = jnp.maximum(block_ids, 0)
    distance = (here - clamped // BLK_DEV) % nodes
    slot_rows = (distance * BLK_DEV + clamped % BLK_DEV) * BT
    for branch in range(branches):
        first_row = branch * BQ
        query_block = turned[first_row : first_row + BQ].reshape(BQ, key_heads, group, HD)
        branch_rows = slot_rows[branch]
        branch_valid = valid[branch]

        def add_slot(slot, state):
            start = branch_rows[slot]
            keys = lax.dynamic_slice_in_dim(window[0], start, BT, 0)
            values = lax.dynamic_slice_in_dim(window[1], start, BT, 0)
            return combine(state, block_terms(query_block, keys, values, branch_valid[slot], None))

        count = SUB
        states[branch] = lax.fori_loop(0, count, add_slot, states[branch])
    outputs = []
    for state in states:
        mixed = state[2] / state[1][..., None]
        outputs.append(mixed.reshape(BQ, heads * HD).astype(jnp.bfloat16))
    attended = jnp.concatenate(outputs, axis=0)
    return lax.all_to_all(attended, "head", split_axis=0, concat_axis=1, tiled=True)


def solution(mesh):
    in_specs = (
        P("node", "head"),
        P(None, "node", "head"),
        P(None, "node", "head"),
        P(None, None, "head"),
        P(),
        P("node"),
    )
    out_specs = P(("node", "head"), None)
    return jax.shard_map(
        per_device, mesh=mesh, in_specs=in_specs, out_specs=out_specs, check_vma=False
    )
```

profile of v0, /device:TPU:1, one launch (start us, length us, event | category | flops | bytes accessed | tf_op | source)
XLA Modules:
  0.0 312.6 jit_solution(4056264591871282808)
XLA Ops:
  0.0 2.4 copy.97
  2.4 2.1 collective-permute-start
  13.4 2.0 fusion.120
  16.5 1.8 fusion.121
  19.0 3.0 subtract_convert_fusion
  26.3 10.6 %collective-permute-done = bf16[2,1024,256]{1,2,0:T(8,128)(2,1)} collective-permute-done((bf16[2,1024,256]{1,2,0:T(8,128)(2,1)}, bf16[2,1024,256]{1,2,0:T(8,128)(2,1)}, u32[]{:S(2)}, u32[]{:S(2)}) %collective-permute-start) | collective-permute-done | bytes 1048608 | tf_op jit(solution)/shard_map/ppermute | solution.py:23
  38.5 2.0 copy-done.4
  41.8 24.6 %collective-permute-done.1 = bf16[2,1024,256]{1,2,0:T(8,128)(2,1)} collective-permute-done((bf16[2,1024,256]{1,2,0:T(8,128)(2,1)}, bf16[2,1024,256]{1,2,0:T(8,128)(2,1)}, u32[]{:S(2)}, u32[]{:S(2)}) %collective-permute-start.1) | collective-permute-done | bytes 1048608 | tf_op jit(solution)/shard_map/ppermute | solution.py:23
  69.8 3.0 fusion.71
  75.6 19.3 %collective-permute-done.2 = bf16[2,1024,256]{1,2,0:T(8,128)(2,1)} collective-permute-done((bf16[2,1024,256]{1,2,0:T(8,128)(2,1)}, bf16[2,1024,256]{1,2,0:T(8,128)(2,1)}, u32[]{:S(2)}, u32[]{:S(2)}) %collective-permute-start.2) | collective-permute-done | bytes 1048608 | tf_op jit(solution)/shard_map/ppermute | solution.py:23
  96.7 1.6 copy.105
  103.5 19.0 %collective-permute-done.3 = bf16[2,1024,256]{1,2,0:T(8,128)(2,1)} collective-permute-done((bf16[2,1024,256]{1,2,0:T(8,128)(2,1)}, bf16[2,1024,256]{1,2,0:T(8,128)(2,1)}, u32[]{:S(2)}, u32[]{:S(2)}) %collective-permute-start.3) | collective-permute-done | bytes 1048608 | tf_op jit(solution)/shard_map/ppermute | solution.py:23
  123.8 2.3 copy-done.2
  126.1 82.4 %while.34 = (s32[]{:T(128)}, f32[128,2,8]{0,2,1:T(8,128)S(1)}, f32[128,2,8]{0,2,1:T(8,128)S(1)}, f32[128,2,8,128]{0,3,2,1:T(8,128)S(1)}, pred[8]{0:T(512)(128)(4...) while((s32[]{:T(128)}, f32[128,2,8]{0,2,1:T(8,128)S(1)}, ...), condition=%wide.region_8.9_spmd, body=%wide.region_5.8_spmd.sunk | while | flops 546320384 | bytes 27377828 | solution.py:144
  128.7 2.9 fusion.162
  134.6 1.8 fusion.165
  139.0 2.9 fusion.162
  144.9 1.8 fusion.165
  149.3 2.9 fusion.162
  155.2 1.8 fusion.165
  159.6 2.9 fusion.162
  165.5 1.8 fusion.165
  169.9 2.9 fusion.162
  175.8 1.8 fusion.165
  180.2 2.9 fusion.162
  186.1 1.8 fusion.165
  190.5 2.9 fusion.162
  196.4 1.8 fusion.165
  200.8 2.9 fusion.162
  206.7 1.8 fusion.165
  208.9 82.4 %while.35 = (s32[]{:T(128)}, f32[128,2,8]{0,2,1:T(8,128)S(1)}, f32[128,2,8]{0,2,1:T(8,128)S(1)}, f32[128,2,8,128]{0,3,2,1:T(8,128)S(1)}, pred[8]{0:T(512)(128)(4...) while((s32[]{:T(128)}, f32[128,2,8]{0,2,1:T(8,128)S(1)}, ...), condition=%wide.region_16.17_spmd, body=%wide.region_13.16_spmd.sunk | while | flops 546320384 | bytes 27377828 | solution.py:144
  211.4 2.9 fusion.170
  217.4 1.8 fusion.173
  221.7 2.9 fusion.170
  227.7 1.8 fusion.173
  232.0 2.9 fusion.170
  238.0 1.8 fusion.173
  242.3 2.9 fusion.170
  248.3 1.8 fusion.173
  252.6 2.9 fusion.170
  258.6 1.8 fusion.173
  262.9 2.9 fusion.170
  268.9 1.8 fusion.173
  273.2 2.9 fusion.170
  279.2 1.8 fusion.173
  283.5 2.9 fusion.170
  289.5 1.8 fusion.173
  291.7 19.8 %all_to_all.19 = bf16[4,64,2048]{2,1,0:T(8,128)(2,1)S(1)} all-to-all(bf16[4,64,2048]{2,1,0:T(8,128)(2,1)S(1)} %bitcast.356), channel_id=1, replica_groups=mesh['node'=64,'head'=4] {'head'}, dimensions={0} | all-to-all | bytes 2097152 | tf_op jit(solution)/shard_map/all_to_all | solution.py:150
  (212 shorter events, 91.8 us)
Async XLA Ops:
  0.0 5.2 %copy-start = (s32[128]{0:T(128)S(1)}, s32[128]{0:T(128)}, u32[]{:S(2)}) copy-start(s32[128]{0:T(128)} %param.14) | copy-start | bytes 1540
  0.0 11.7 %copy-start.17 = (s32[2]{0:T(128)S(1)}, s32[2]{0:T(128)}, u32[]{:S(2)}) copy-start(s32[2]{0:T(128)} %param.15) | copy-start | bytes 28
  0.0 12.7 %copy-start.7 = (bf16[256,2048]{1,0:T(8,128)(2,1)S(1)}, bf16[256,2048]{1,0:T(8,128)(2,1)}, u32[]{:S(2)}) copy-start(bf16[256,2048]{1,0:T(8,128)(2,1)} %param.10) | copy-start | bytes 3145732
  2.4 34.5 %collective-permute-start = (bf16[2,1024,256]{1,2,0:T(8,128)(2,1)}, bf16[2,1024,256]{1,2,0:T(8,128)(2,1)}, u32[]{:S(2)}, u32[]{:S(2)}) collective-permute-start(bf16[2,1024,256]{1,2,0:T(8,128)(2,1)} %copy.97), channel_id=1, source_target_pairs={{0,4},{4,8},{8,12},{12,16},{16,20},{20,24},{24,28},{28,32},{32,36}... | collective-permute-start | bytes 3145736 | tf_op jit(solution)/shard_map/ppermute | solution.py:23
  13.4 2.0 slice-start
  19.0 3.6 %copy-start.8 = (f32[256,2,64]{2,0,1:T(8,128)S(1)}, f32[256,2,64]{2,0,1:T(8,128)}, u32[]{:S(2)}) copy-start(f32[256,2,64]{2,0,1:T(8,128)} %copy.147) | copy-start | bytes 393220
  23.4 2.8 copy-start.3
  23.8 13.3 %copy-start.9 = (bf16[2,256,256]{2,1,0:T(8,128)(2,1)S(1)}, bf16[2,256,256]{2,1,0:T(8,128)(2,1)}, u32[]{:S(2)}) copy-start(bf16[2,256,256]{2,1,0:T(8,128)(2,1)} %param.11) | copy-start | bytes 786436
  36.9 29.5 %collective-permute-start.1 = (bf16[2,1024,256]{1,2,0:T(8,128)(2,1)}, bf16[2,1024,256]{1,2,0:T(8,128)(2,1)}, u32[]{:S(2)}, u32[]{:S(2)}) collective-permute-start(bf16[2,1024,256]{1,2,0:T(8,128)(2,1)} %collective-permute-done), channel_id=1, source_target_pairs={{0,4},{4,8},{8,12},{12,16},{16,20},{20,24},{24,28},{28,32},{32,36}... | collective-permute-start | bytes 3145736 | tf_op jit(solution)/shard_map/ppermute | solution.py:23
  37.7 32.0 %copy-start.12 = (f32[128,2,8]{0,2,1:T(8,128)S(1)}, f32[128,2,8]{0,2,1:T(8,128)}, u32[]{:S(2)}) copy-start(f32[128,2,8]{0,2,1:T(8,128)} %get-tuple-element.394) | copy-start | bytes 24580
  38.5 2.0 copy-start.4
  41.8 31.1 %copy-start.11 = (f32[128,2,8]{0,2,1:T(8,128)S(1)}, f32[128,2,8]{0,2,1:T(8,128)}, u32[]{:S(2)}) copy-start(f32[128,2,8]{0,2,1:T(8,128)} %get-tuple-element.395) | copy-start | bytes 24580
  66.4 28.5 %collective-permute-start.2 = (bf16[2,1024,256]{1,2,0:T(8,128)(2,1)}, bf16[2,1024,256]{1,2,0:T(8,128)(2,1)}, u32[]{:S(2)}, u32[]{:S(2)}) collective-permute-start(bf16[2,1024,256]{1,2,0:T(8,128)(2,1)} %collective-permute-done.1), channel_id=1, source_target_pairs={{0,4},{4,8},{8,12},{12,16},{16,20},{20,24},{24,28},{28,32},{32,36}... | collective-permute-start | bytes 3145736 | tf_op jit(solution)/shard_map/ppermute | solution.py:23
  69.8 3.1 copy-start.10
  69.8 4.6 %copy-start.5 = (f32[2,128,8,512]{3,1,2,0:T(8,128)S(1)}, f32[2,128,8,512]{3,1,2,0:T(8,128)}, u32[]{:S(2)}) copy-start(f32[2,128,8,512]{3,1,2,0:T(8,128)} %copy-done.4) | copy-start | bytes 12582916
  69.8 4.6 %copy-start.14 = (f32[128,2,8]{0,2,1:T(8,128)S(1)}, f32[128,2,8]{0,2,1:T(8,128)}, u32[]{:S(2)}) copy-start(f32[128,2,8]{0,2,1:T(8,128)} %get-tuple-element.397) | copy-start | bytes 24580
  72.8 22.1 %copy-start.13 = (f32[128,2,8]{0,2,1:T(8,128)S(1)}, f32[128,2,8]{0,2,1:T(8,128)}, u32[]{:S(2)}) copy-start(f32[128,2,8]{0,2,1:T(8,128)} %get-tuple-element.398) | copy-start | bytes 24580
  74.3 22.1 %copy-start.6 = (f32[128,2,8,128]{3,0,2,1:T(8,128)S(1)}, f32[128,2,8,128]{3,0,2,1:T(8,128)}, u32[]{:S(2)}) copy-start(f32[128,2,8,128]{3,0,2,1:T(8,128)} %fusion.65) | copy-start | bytes 3145732
  94.9 27.6 %collective-permute-start.3 = (bf16[2,1024,256]{1,2,0:T(8,128)(2,1)}, bf16[2,1024,256]{1,2,0:T(8,128)(2,1)}, u32[]{:S(2)}, u32[]{:S(2)}) collective-permute-start(bf16[2,1024,256]{1,2,0:T(8,128)(2,1)} %collective-permute-done.2), channel_id=1, source_target_pairs={{0,4},{4,8},{8,12},{12,16},{16,20},{20,24},{24,28},{28,32},{32,36}... | collective-permute-start | bytes 3145736 | tf_op jit(solution)/shard_map/ppermute | solution.py:23
  94.9 4.7 %copy-start.15 = (pred[2,8]{1,0:T(4,128)(4,1)S(1)}, pred[2,8]{1,0:T(4,128)(4,1)}, u32[]{:S(2)}) copy-start(pred[2,8]{1,0:T(4,128)(4,1)} %get-tuple-element.400) | copy-start | bytes 52
  94.9 4.7 %copy-start.16 = (s32[2,8]{1,0:T(2,128)S(1)}, s32[2,8]{1,0:T(2,128)}, u32[]{:S(2)}) copy-start(s32[2,8]{1,0:T(2,128)} %get-tuple-element.439) | copy-start | bytes 196
  123.8 2.3 copy-start.2
  291.3 21.3 %copy-start.1 = (s32[128]{0:T(128)S(1)}, s32[128]{0:T(128)}, u32[]{:S(2)}) copy-start(s32[128]{0:T(128)} %param.14) | copy-start | bytes 1540
where the time goes:
time: 314 us; the launch traced here: 313 us
  local copies, waits for them, and re-layouts  100 us (32%)
  waiting for transfers between devices  73.5 us (23%)
  matrix products  51 us (16%)
  other arithmetic  33.5 us (11%)
  loops' own time  31.9 us (10%)
  blocking collectives  19.8 us (6%)
    ppermute x4, waiting for transfers between devices, from_behind(): return lax.ppermute(value, axis, pairs)  73.5 us
    slice x16, local copies, waits for them, and re-layouts, add_slot(): values = lax.dynamic_slice_in_dim(window[1], start, BT, 0)  46 us
    dot_general x20, matrix products, block_terms(): jnp.einsum('hgqn,nhd->qhgd', weights.astype(jnp.bfloat16), value_heads, p...  36.4 us
    another operation x2, loops' own time, per_device(): states[branch] = lax.fori_loop(0, count, add_slot, states[branch])  31.9 us
    all_to_all x1, blocking collectives, per_device(): lax.all_to_all(attended, 'head', split_axis=0, concat_axis=1, tiled=True)  19.8 us
    unnamed x49, local copies, waits for them, and re-layouts  16.2 us
    dot_general x20, matrix products, block_terms(): jnp.einsum('qhgd,nhd->hgqn', query_block, key_heads, preferred_element_ty...  14.6 us
    reduce_sum x20, other arithmetic, block_terms(): total = jnp.sum(weights, axis=-1)  14.1 us
  transfers between devices with their start and end apart: 4, of which 4 were waited for; matrix products, arithmetic and copies ran while one was open for 13% of the time, Pallas kernels for 0%

commit v1 on v0

v1 whole, which is shorter than its diff:
```python
import math

import jax
import jax.numpy as jnp
import numpy as np
from jax import lax
from jax.experimental import pallas as pl
from jax.experimental.pallas import tpu as pltpu
from jax.sharding import PartitionSpec as P

HD = 128
BT = 512
BQ = 128
SUB = 8
BLK_DEV = 2
BR_DEV = 2
RING = 4
GROUP = 8
COLS = GROUP * BQ
TILE = 256
AHEAD = 2
LAG = 1
ONES = 16

BASE = 1000000.0
NEG = -1e30
MESH = pl.DeviceIdType.MESH

SHARED = 2
FAR = 3
FAR_EVEN = 10
SLOTS = 11
FIRST = 3
REMOTE = 7
BACK = {0: 0, 1: -1, 3: 7, 4: 2, 5: 1, 6: 6, 7: 5, 8: 4, 9: 3}
BEHIND = {4: 2, 5: 1, 6: 6, 7: 5, 8: 4, 9: 3, 3: 7, 0: 0, 1: -1}


def attention_kernel(
    nodes,
    parent,
    leaf,
    inverse,
    queries,
    own_cache,
    tree_cache,
    shared_cache,
    out,
    raw,
    turned,
    own,
    own_keys,
    kbuf,
    vbuf,
    peaks,
    totals,
    acc,
    obuf,
    live,
    load_sem,
    own_sem,
    local_k,
    local_v,
    z_send,
    up_send,
    down_send,
    relay_up_send,
    relay_down_send,
    recv_k,
    recv_v,
    out_send,
    out_recv,
    out_local,
):
    node = lax.axis_index("node")
    head = lax.axis_index("head")
    heads = 4
    y = lax.rem(node, RING)
    plane = node - y
    up = plane + lax.rem(y + 1, RING)
    down = plane + lax.rem(y + RING - 1, RING)
    after = lax.rem(node + 1, nodes)
    before = lax.rem(node + nodes - 1, nodes)
    ahead = lax.rem(node + RING, nodes)
    behind = lax.rem(node + nodes - RING, nodes)
    others = [lax.rem(head + k, heads) for k in range(1, heads)]

    def local_tree(g, blk):
        rows = pl.ds(blk * BT, BT)
        columns = pl.ds(g * HD, HD)
        return (
            pltpu.make_async_copy(tree_cache.at[0, rows, columns], kbuf.at[g, blk], local_k.at[g, blk]),
            pltpu.make_async_copy(tree_cache.at[1, rows, columns], vbuf.at[g, blk], local_v.at[g, blk]),
        )

    def local_shared(g):
        columns = pl.ds(g * HD, HD)
        return (
            pltpu.make_async_copy(shared_cache.at[0, :, columns], kbuf.at[g, SHARED], local_k.at[g, SHARED]),
            pltpu.make_async_copy(shared_cache.at[1, :, columns], vbuf.at[g, SHARED], local_v.at[g, SHARED]),
        )

    load_queries = pltpu.make_async_copy(queries, raw, load_sem)
    load_own = pltpu.make_async_copy(own_cache, own, own_sem)
    for g in range(2):
        for blk in range(2):
            for copy in local_tree(g, blk):
                copy.start()
    load_queries.start()
    load_own.start()
    for g in range(2):
        for copy in local_shared(g):
            copy.start()

    barrier = pltpu.get_barrier_semaphore()
    for source in (down, up, behind, before, after):
        pl.semaphore_signal(barrier, inc=1, device_id=(source, head), device_id_type=MESH)
    for other in others:
        pl.semaphore_signal(barrier, inc=1, device_id=(node, other), device_id_type=MESH)
    pl.semaphore_wait(barrier, 8)

    bufs = (kbuf, vbuf)
    recvs = (recv_k, recv_v)

    def remote(kv, g, source, target, sem, device):
        return pltpu.make_async_remote_copy(
            src_ref=bufs[kv].at[g, source],
            dst_ref=bufs[kv].at[g, target],
            send_sem=sem,
            recv_sem=recvs[kv].at[g, target],
            device_id=(device, head),
            device_id_type=MESH,
        )

    far_slot = (FAR_EVEN, FAR)
    passes_up = y == RING - 1
    passes_down = y > 0

    def z_copy(g, kv, blk):
        return remote(kv, g, blk, far_slot[blk], z_send.at[g, kv, blk], ahead)

    def up_copy(g, kv, blk):
        source = jnp.where(passes_up, far_slot[blk], blk)
        return remote(kv, g, source, 4 + blk, up_send.at[g, kv, blk], up)

    def down_copy(g, kv, blk):
        source = jnp.where(passes_down, far_slot[blk], blk)
        return remote(kv, g, source, 6 + blk, down_send.at[g, kv, blk], down)

    def relay_up(g, blk):
        return remote(0, g, 4 + blk, 8 + blk, relay_up_send.at[g, blk], after)

    def relay_down(g, blk):
        return remote(1, g, 6 + blk, 8 + blk, relay_down_send.at[g, blk], before)

    def arrived(g, kv, slot):
        pltpu.make_async_copy(bufs[kv].at[g, slot], bufs[kv].at[g, slot], recvs[kv].at[g, slot]).wait()

    chunks = ((0, 1), (1, 1), (0, 0), (1, 0))

    def send_own(g):
        for kv, blk in chunks:
            z_copy(g, kv, blk).start()

            @pl.when(jnp.logical_not(passes_up))
            def _():
                up_copy(g, kv, blk).start()

            @pl.when(jnp.logical_not(passes_down))
            def _():
                down_copy(g, kv, blk).start()

    def forward(g, chunk):
        kv, blk = chunks[chunk]
        arrived(g, kv, far_slot[blk])

        @pl.when(passes_down)
        def _():
            down_copy(g, kv, blk).start()

        @pl.when(passes_up)
        def _():
            up_copy(g, kv, blk).start()

    def pass_up(g, blk):
        arrived(g, 0, 4 + blk)
        relay_up(g, blk).start()

    def pass_down(g, blk):
        arrived(g, 1, 6 + blk)
        relay_down(g, blk).start()

    for g in range(2):
        for blk in range(2):
            for copy in local_tree(g, blk):
                copy.wait()
    send_own(0)

    ids = {slot: lax.rem(node * BLK_DEV + nodes * BLK_DEV - back, nodes * BLK_DEV) for slot, back in BACK.items()}
    depths = []
    for b in range(BR_DEV):
        current = leaf[b]
        depth = jnp.int32(0)
        hits = {slot: jnp.int32(0) for slot in ids}
        for step in range(SUB):
            valid = current >= 0
            depth = depth + valid.astype(jnp.int32)
            for slot, block in ids.items():
                hits[slot] = hits[slot] + (current == block).astype(jnp.int32)
            current = jnp.where(valid, parent[jnp.maximum(current, 0)], -1)
        depths.append(depth)
        for slot in ids:
            live[b, slot] = hits[slot]
        live[b, SHARED] = jnp.int32(1)

    load_queries.wait()
    load_own.wait()
    offsets = lax.broadcasted_iota(jnp.int32, (BQ, HD), 0)
    lane = lax.broadcasted_iota(jnp.int32, (BQ, HD), 1)
    factor = math.log2(math.e) / math.sqrt(HD)
    for b in range(BR_DEV):
        position = BT * (depths[b] + 1) + offsets
        angle = position.astype(jnp.float32) * inverse[...]
        cosine = jnp.cos(angle)
        sine = jnp.sin(angle)
        sine = jnp.where(lane < HD // 2, -sine, sine)

        def rotate(field):
            return field * cosine + pltpu.roll(field, HD // 2, 1) * sine

        rows = pl.ds(b * BQ, BQ)
        for g in range(2):
            for h in range(GROUP):
                field = raw[rows, (g * GROUP + h) * HD : (g * GROUP + h + 1) * HD].astype(jnp.float32)
                turned[g, b, h * BQ : (h + 1) * BQ, :] = (rotate(field) * factor).astype(jnp.bfloat16)
            field = own[0, rows, g * HD : (g + 1) * HD].astype(jnp.float32)
            own_keys[g, b] = rotate(field).astype(jnp.bfloat16)

    def scores_of(keys, g, b, r):
        return lax.dot_general(
            keys,
            turned[g, b, r : r + TILE, :],
            (((1,), (1,)), ((), ())),
            preferred_element_type=jnp.float32,
        )

    def with_ones(values):
        return jnp.concatenate([values.T, jnp.ones((ONES, values.shape[0]), jnp.bfloat16)], axis=0)

    def weigh(values, weights):
        return lax.dot_general(
            values, weights, (((1,), (0,)), ((), ())), preferred_element_type=jnp.float32
        )

    for g in range(2):
        for b in range(BR_DEV):
            keys = own_keys[g, b]
            values = with_ones(own[1, b * BQ : (b + 1) * BQ, g * HD : (g + 1) * HD])
            for r in range(0, COLS, TILE):
                scores = scores_of(keys, g, b, r)
                key_at = lax.broadcasted_iota(jnp.int32, (BQ, TILE), 0)
                token = lax.rem(lax.broadcasted_iota(jnp.int32, (BQ, TILE), 1), BQ)
                scores = jnp.where(key_at <= token, scores, NEG)
                peak = jnp.max(scores, axis=0, keepdims=True)
                weights = jnp.exp2(scores - peak).astype(jnp.bfloat16)
                mixed = weigh(values, weights)
                peaks[g, b, 0:1, r : r + TILE] = peak
                totals[g, b, 0:1, r : r + TILE] = mixed[HD : HD + 1]
                acc[g, b, :, r : r + TILE] = mixed[:HD]

    tiles = [(b, r) for b in range(BR_DEV) for r in range(0, COLS, TILE)]

    def attend(g, slot):
        keys = kbuf[g, slot]
        values = with_ones(vbuf[g, slot])
        on = [live[b, slot] > 0 for b in range(BR_DEV)]

        def soften(b, r, scores):
            before_peak = peaks[g, b, 0:1, r : r + TILE]
            peak = jnp.maximum(before_peak, jnp.where(on[b], jnp.max(scores, axis=0, keepdims=True), NEG))
            peaks[g, b, 0:1, r : r + TILE] = peak
            shift = jnp.where(on[b], peak, -NEG)
            weights = jnp.exp2(scores - shift).astype(jnp.bfloat16)
            return weights, jnp.exp2(before_peak - peak)

        def add(b, r, weights, fade):
            mixed = weigh(values, weights)
            acc[g, b, :, r : r + TILE] = acc[g, b, :, r : r + TILE] * fade + mixed[:HD]
            totals[g, b, 0:1, r : r + TILE] = totals[g, b, 0:1, r : r + TILE] * fade + mixed[HD : HD + 1]

        ready = [scores_of(keys, g, *tile) for tile in tiles[:AHEAD]]
        waiting = []
        for at, tile in enumerate(tiles):
            if at + AHEAD < len(tiles):
                ready.append(scores_of(keys, g, *tiles[at + AHEAD]))
            waiting.append(tile + soften(*tile, ready[at]))
            ready[at] = None
            if len(waiting) > LAG:
                add(*waiting.pop(0))
        for item in waiting:
            add(*item)

    def finish(g):
        for b in range(BR_DEV):
            for h in range(GROUP):
                span = slice(h * BQ, (h + 1) * BQ)
                mixed = acc[g, b, :, span] / totals[g, b, 0:1, span]
                obuf[b * BQ : (b + 1) * BQ, (g * GROUP + h) * HD : (g * GROUP + h + 1) * HD] = mixed.T.astype(
                    jnp.bfloat16
                )

    part = BR_DEV * BQ // heads

    def out_copy(g, k):
        device = others[k - 1]
        return pltpu.make_async_remote_copy(
            src_ref=obuf.at[pl.ds(pl.multiple_of(device * part, part), part), pl.ds(g * COLS, COLS)],
            dst_ref=out.at[:, pl.ds(pl.multiple_of((head * 2 + g) * COLS, COLS), COLS)],
            send_sem=out_send.at[g, k - 1],
            recv_sem=out_recv.at[g, k - 1],
            device_id=(node, device),
            device_id_type=MESH,
        )

    def out_keep(g):
        return pltpu.make_async_copy(
            obuf.at[pl.ds(pl.multiple_of(head * part, part), part), pl.ds(g * COLS, COLS)],
            out.at[:, pl.ds(pl.multiple_of((head * 2 + g) * COLS, COLS), COLS)],
            out_local.at[g],
        )

    def exchange(g):
        for k in (2, 1, 3):
            out_copy(g, k).start()
        out_keep(g).start()

    for g in range(2):
        for copy in local_shared(g):
            copy.wait()

    def local_step(i, carry):
        attend(i // 3, lax.rem(i, 3))

        @pl.when(i == 0)
        def _():
            forward(0, 0)

        @pl.when(i == 1)
        def _():
            forward(0, 1)
            pass_up(0, 1)

        @pl.when(i == 2)
        def _():
            pass_down(0, 1)

        @pl.when(i == 3)
        def _():
            forward(0, 2)
            send_own(1)

        @pl.when(i == 4)
        def _():
            forward(0, 3)
            pass_up(0, 0)

        @pl.when(i == 5)
        def _():
            pass_down(0, 0)

        return carry

    lax.fori_loop(0, 6, local_step, 0)

    def first_step(i, carry):
        slot = FIRST + i

        @pl.when((i == 1) | (i == 2))
        def _():
            arrived(0, 1, slot)

        @pl.when((i == 3) | (i == 4))
        def _():
            arrived(0, 0, slot)

        @pl.when(i >= 5)
        def _():
            arrived(0, 0, slot)
            arrived(0, 1, slot)

        @pl.when(i == 2)
        def _():
            forward(1, 0)

        @pl.when(i == 3)
        def _():
            forward(1, 1)
            pass_up(1, 1)

        @pl.when(i == 4)
        def _():
            pass_down(1, 1)

        @pl.when(i == 5)
        def _():
            forward(1, 2)

        @pl.when(i == 6)
        def _():
            forward(1, 3)

        attend(0, slot)
        return carry

    lax.fori_loop(0, REMOTE, first_step, 0)
    pass_up(1, 0)
    pass_down(1, 0)
    finish(0)
    exchange(0)

    def second_step(i, carry):
        slot = FIRST + i

        @pl.when((i == 1) | (i == 2))
        def _():
            arrived(1, 1, slot)

        @pl.when((i == 3) | (i == 4))
        def _():
            arrived(1, 0, slot)

        @pl.when(i >= 5)
        def _():
            arrived(1, 0, slot)
            arrived(1, 1, slot)

        attend(1, slot)
        return carry

    lax.fori_loop(0, REMOTE, second_step, 0)
    finish(1)
    exchange(1)

    for g in range(2):
        for kv, blk in chunks:
            z_copy(g, kv, blk).wait_send()
            up_copy(g, kv, blk).wait_send()
            down_copy(g, kv, blk).wait_send()
        for blk in range(2):
            relay_up(g, blk).wait_send()
            relay_down(g, blk).wait_send()
        for k in range(1, heads):
            out_copy(g, k).wait()
        out_keep(g).wait()


def inverse_frequencies():
    half = HD // 2
    inverse = np.power(np.float64(BASE), -np.arange(half) * (2.0 / HD)).astype(np.float32)
    return np.concatenate([inverse, inverse])[None, :]


def per_device(queries, own_cache, tree_cache, shared_cache, parent, leaf):
    nodes = lax.axis_size("node")
    heads = lax.axis_size("head")
    rows = queries.shape[0]
    dma = pltpu.SemaphoreType.DMA
    anywhere = pl.BlockSpec(memory_space=pl.ANY)
    scalars = pl.BlockSpec(memory_space=pltpu.SMEM)

    def kernel(*refs):
        attention_kernel(nodes, *refs)

    return pl.pallas_call(
        kernel,
        out_shape=jax.ShapeDtypeStruct((rows // heads, queries.shape[1] * heads), jnp.bfloat16),
        in_specs=[
            scalars,
            scalars,
            pl.BlockSpec(memory_space=pltpu.VMEM),
            anywhere,
            anywhere,
            anywhere,
            anywhere,
        ],
        out_specs=anywhere,
        scratch_shapes=[
            pltpu.VMEM(queries.shape, jnp.bfloat16),
            pltpu.VMEM((2, BR_DEV, COLS, HD), jnp.bfloat16),
            pltpu.VMEM(own_cache.shape, jnp.bfloat16),
            pltpu.VMEM((2, BR_DEV, BQ, HD), jnp.bfloat16),
            pltpu.VMEM((2, SLOTS, BT, HD), jnp.bfloat16),
            pltpu.VMEM((2, SLOTS, BT, HD), jnp.bfloat16),
            pltpu.VMEM((2, BR_DEV, 8, COLS), jnp.float32),
            pltpu.VMEM((2, BR_DEV, 8, COLS), jnp.float32),
            pltpu.VMEM((2, BR_DEV, HD, COLS), jnp.float32),
            pltpu.VMEM(queries.shape, jnp.bfloat16),
            pltpu.SMEM((BR_DEV, 16), jnp.int32),
            dma,
            dma,
            dma((2, 3)),
            dma((2, 3)),
            dma((2, 2, 2)),
            dma((2, 2, 2)),
            dma((2, 2, 2)),
            dma((2, 2)),
            dma((2, 2)),
            dma((2, SLOTS)),
            dma((2, SLOTS)),
            dma((2, 3)),
            dma((2, 3)),
            dma((2,)),
        ],
        compiler_params=pltpu.CompilerParams(
            collective_id=0, has_side_effects=True, vmem_limit_bytes=48 * 1024 * 1024
        ),
        name="branch_attention",
    )(parent, leaf, jnp.asarray(inverse_frequencies()), queries, own_cache, tree_cache, shared_cache)


def solution(mesh):
    in_specs = (
        P("node", "head"),
        P(None, "node", "head"),
        P(None, "node", "head"),
        P(None, None, "head"),
        P(),
        P("node"),
    )
    out_specs = P(("node", "head"), None)
    return jax.shard_map(
        per_device, mesh=mesh, in_specs=in_specs, out_specs=out_specs, check_vma=False
    )
```

time: 314 us -> 78.1 us (0.25)
  local copies, waits for them, and re-layouts: 100 us -> 7.38 us
  waiting for transfers between devices: 73.5 us -> 0 us
  Pallas kernels: 0 us -> 70.4 us
  matrix products: 51 us -> 0 us
  other arithmetic: 33.5 us -> 0 us
  loops' own time: 31.9 us -> 0 us
  blocking collectives: 19.8 us -> 0 us
    ppermute x4 -> x0, waiting for transfers between devices: 73.5 us -> none  [from_behind(): return lax.ppermute(value, axis, pairs)]
    pallas_call x0 -> x1, Pallas kernels: none -> 70.4 us  [per_device(): pl.pallas_call(kernel, out_shape=jax.ShapeDtypeStruct((rows // heads, que...]
    dot_general x40 -> x0, matrix products: 51 us -> none  [the longest x20 36.4 us: block_terms(): jnp.einsum('hgqn,nhd->qhgd', weights.astype(jnp.bfloat16), value_heads, p...]
    slice x22 -> x0, local copies, waits for them, and re-layouts: 50.4 us -> none  [the longest x16 46 us: add_slot(): values = lax.dynamic_slice_in_dim(window[1], start, BT, 0)]
    another operation x2 -> x0, loops' own time: 31.9 us -> none  [per_device(): states[branch] = lax.fori_loop(0, count, add_slot, states[branch])]
    dynamic_slice x48 -> x0, local copies, waits for them, and re-layouts: 23.8 us -> none  [the longest x16 9.46 us: add_slot(): branch_valid[slot]]
    all_to_all x1 -> x0, blocking collectives: 19.8 us -> none  [per_device(): lax.all_to_all(attended, 'head', split_axis=0, concat_axis=1, tiled=True)]
    reduce_sum x21 -> x0, other arithmetic: 14.8 us -> none  [the longest x20 14.1 us: block_terms(): total = jnp.sum(weights, axis=-1)]
  transfers between devices with their start and end apart: 4 -> 0, of which waited for: 4 -> 0; matrix products, arithmetic and copies ran while one was open for 13% -> 0% of each run, Pallas kernels for 0% -> 0%
where the time goes in v1:
time: 78.1 us; the launch traced here: 77.8 us
  Pallas kernels  70.4 us (90%)
  local copies, waits for them, and re-layouts  7.38 us (9%)
    pallas_call x1, Pallas kernels, per_device(): pl.pallas_call(kernel, out_shape=jax.ShapeDtypeStruct((rows // heads, que...  70.4 us
    unnamed x15, local copies, waits for them, and re-layouts  7.38 us

profile of v1, /device:TPU:1, one launch (start us, length us, event | category | flops | bytes accessed | tf_op | source)
XLA Modules:
  0.0 77.8 jit_solution(17593789857129017126)
XLA Ops:
  0.0 0.0 copy-start
  0.0 1.2 %copy-done = bf16[256,2048]{1,0:T(8,128)(2,1)S(1)} copy-done((bf16[256,2048]{1,0:T(8,128)(2,1)S(1)}, bf16[256,2048]{1,0:T(8,128)(2,1)}, u32[]{:S(2)}) %copy-start) | copy-done | bytes 1048600
  1.2 0.0 copy-start.1
  1.2 1.2 %copy-done.1 = bf16[2,1024,256]{2,1,0:T(8,128)(2,1)S(1)} copy-done((bf16[2,1024,256]{2,1,0:T(8,128)(2,1)S(1)}, bf16[2,1024,256]{2,1,0:T(8,128)(2,1)}, u32[]{:S(2)}) %copy-start.1) | copy-done | bytes 1048600
  2.5 0.0 copy-start.2
  2.5 1.0 %copy-done.2 = bf16[2,512,256]{2,1,0:T(8,128)(2,1)S(1)} copy-done((bf16[2,512,256]{2,1,0:T(8,128)(2,1)S(1)}, bf16[2,512,256]{2,1,0:T(8,128)(2,1)}, u32[]{:S(2)}) %copy-start.2) | copy-done | bytes 524312
  3.5 0.0 copy-start.3
  3.5 0.9 %copy-done.3 = bf16[2,256,256]{2,1,0:T(8,128)(2,1)S(1)} copy-done((bf16[2,256,256]{2,1,0:T(8,128)(2,1)S(1)}, bf16[2,256,256]{2,1,0:T(8,128)(2,1)}, u32[]{:S(2)}) %copy-start.3) | copy-done | bytes 262168
  4.4 0.0 copy-start.4
  4.4 0.7 copy-done.4
  5.1 0.0 copy-start.5
  5.1 0.7 copy-done.5
  5.8 0.0 copy-start.6
  5.8 0.7 copy-done.6
  6.4 70.4 %branch_attention.1 = bf16[64,8192]{1,0:T(8,128)(2,1)S(1)} custom-call(s32[128]{0:T(128)S(1)} %copy-done.4, s32[2]{0:T(128)S(1)} %copy-done.5, f32[1,128]{1,0:T(1,128)S(1)} %copy-done.6, bf16[256,2048]{1,0:T(8,128)(2,1)S(1)} %copy-done, bf16[2,256,256]{2,1,0:T(8,128)(2,1)S(1)} %copy-done.3, bf16[2,1024,256]{2,1,0:T(8,128)(2,1)S(1)} %copy-done.1, ...), custom_call_target="tpu_custom_call" | custom-call | tf_op jit(solution)/shard_map/branch_attention/pallas_call | solution.py:474
  76.9 1.0 %copy.9 = bf16[64,8192]{1,0:T(8,128)(2,1)} copy(bf16[64,8192]{1,0:T(8,128)(2,1)S(1)} %branch_attention.1) | data formatting | bytes 2097152
Async XLA Ops:
  0.0 1.2 %copy-start = (bf16[256,2048]{1,0:T(8,128)(2,1)S(1)}, bf16[256,2048]{1,0:T(8,128)(2,1)}, u32[]{:S(2)}) copy-start(bf16[256,2048]{1,0:T(8,128)(2,1)} %refs_3_.1) | copy-start | bytes 3145732
  1.2 1.2 %copy-start.1 = (bf16[2,1024,256]{2,1,0:T(8,128)(2,1)S(1)}, bf16[2,1024,256]{2,1,0:T(8,128)(2,1)}, u32[]{:S(2)}) copy-start(bf16[2,1024,256]{2,1,0:T(8,128)(2,1)} %refs_5_.1) | copy-start | bytes 3145732
  2.5 1.0 %copy-start.2 = (bf16[2,512,256]{2,1,0:T(8,128)(2,1)S(1)}, bf16[2,512,256]{2,1,0:T(8,128)(2,1)}, u32[]{:S(2)}) copy-start(bf16[2,512,256]{2,1,0:T(8,128)(2,1)} %refs_6_.1) | copy-start | bytes 1572868
  3.5 0.9 %copy-start.3 = (bf16[2,256,256]{2,1,0:T(8,128)(2,1)S(1)}, bf16[2,256,256]{2,1,0:T(8,128)(2,1)}, u32[]{:S(2)}) copy-start(bf16[2,256,256]{2,1,0:T(8,128)(2,1)} %refs_4_.1) | copy-start | bytes 786436
  4.4 0.7 copy-start.4
  5.1 0.7 copy-start.5
  5.8 0.7 copy-start.6

commit v2 on v1

--- a/solution.py
+++ b/solution.py
@@ -27,20 +27,21 @@
 MESH = pl.DeviceIdType.MESH
 
 SHARED = 2
-FAR = 3
-FAR_EVEN = 10
+FAR = (10, 3)
+NEXT = (5, 4)
+THIRD = (9, 6)
+SECOND = (8, 7)
 SLOTS = 11
 FIRST = 3
 REMOTE = 7
-BACK = {0: 0, 1: -1, 3: 7, 4: 2, 5: 1, 6: 6, 7: 5, 8: 4, 9: 3}
-BEHIND = {4: 2, 5: 1, 6: 6, 7: 5, 8: 4, 9: 3, 3: 7, 0: 0, 1: -1}
+BACK = {0: 0, 1: -1, 3: 7, 4: 1, 5: 2, 6: 5, 9: 6, 7: 3, 8: 4}
 
 
 def attention_kernel(
     nodes,
-    parent,
-    leaf,
-    inverse,
+    parent_in,
+    leaf_in,
+    inverse_in,
     queries,
     own_cache,
     tree_cache,
@@ -56,7 +57,11 @@
     totals,
     acc,
     obuf,
+    parent,
+    leaf,
+    inverse,
     live,
+    small_sem,
     load_sem,
     own_sem,
     local_k,
@@ -106,6 +111,13 @@
         for blk in range(2):
             for copy in local_tree(g, blk):
                 copy.start()
+    small = [
+        pltpu.make_async_copy(parent_in, parent, small_sem.at[0]),
+        pltpu.make_async_copy(leaf_in, leaf, small_sem.at[1]),
+        pltpu.make_async_copy(inverse_in, inverse, small_sem.at[2]),
+    ]
+    for copy in small:
+        copy.start()
     load_queries.start()
     load_own.start()
     for g in range(2):
@@ -132,47 +144,57 @@
             device_id_type=MESH,
         )
 
-    far_slot = (FAR_EVEN, FAR)
     passes_up = y == RING - 1
     passes_down = y > 0
 
     def z_copy(g, kv, blk):
-        return remote(kv, g, blk, far_slot[blk], z_send.at[g, kv, blk], ahead)
+        return pltpu.make_async_remote_copy(
+            src_ref=tree_cache.at[kv, pl.ds(blk * BT, BT), pl.ds(g * HD, HD)],
+            dst_ref=bufs[kv].at[g, FAR[blk]],
+            send_sem=z_send.at[g, kv, blk],
+            recv_sem=recvs[kv].at[g, FAR[blk]],
+            device_id=(ahead, head),
+            device_id_type=MESH,
+        )
 
     def up_copy(g, kv, blk):
-        source = jnp.where(passes_up, far_slot[blk], blk)
-        return remote(kv, g, source, 4 + blk, up_send.at[g, kv, blk], up)
+        source = jnp.where(passes_up, FAR[blk], blk)
+        return remote(kv, g, source, NEXT[blk], up_send.at[g, kv, blk], up)
 
     def down_copy(g, kv, blk):
-        source = jnp.where(passes_down, far_slot[blk], blk)
-        return remote(kv, g, source, 6 + blk, down_send.at[g, kv, blk], down)
+        source = jnp.where(passes_down, FAR[blk], blk)
+        return remote(kv, g, source, THIRD[blk], down_send.at[g, kv, blk], down)
 
     def relay_up(g, blk):
-        return remote(0, g, 4 + blk, 8 + blk, relay_up_send.at[g, blk], after)
+        return remote(0, g, NEXT[blk], SECOND[blk], relay_up_send.at[g, blk], after)
 
     def relay_down(g, blk):
-        return remote(1, g, 6 + blk, 8 + blk, relay_down_send.at[g, blk], before)
+        return remote(1, g, THIRD[blk], SECOND[blk], relay_down_send.at[g, blk], before)
 
     def arrived(g, kv, slot):
         pltpu.make_async_copy(bufs[kv].at[g, slot], bufs[kv].at[g, slot], recvs[kv].at[g, slot]).wait()
 
-    chunks = ((0, 1), (1, 1), (0, 0), (1, 0))
+    values_first = ((1, 1), (1, 0), (0, 1), (0, 0))
+    keys_first = ((0, 1), (0, 0), (1, 1), (1, 0))
+
+    def send_far(g):
+        for kv, blk in values_first:
+            z_copy(g, kv, blk).start()
 
     def send_own(g):
-        for kv, blk in chunks:
-            z_copy(g, kv, blk).start()
-
-            @pl.when(jnp.logical_not(passes_up))
-            def _():
+        @pl.when(jnp.logical_not(passes_up))
+        def _():
+            for kv, blk in keys_first:
                 up_copy(g, kv, blk).start()
 
-            @pl.when(jnp.logical_not(passes_down))
-            def _():
+        @pl.when(jnp.logical_not(passes_down))
+        def _():
+            for kv, blk in values_first:
                 down_copy(g, kv, blk).start()
 
     def forward(g, chunk):
-        kv, blk = chunks[chunk]
-        arrived(g, kv, far_slot[blk])
+        kv, blk = values_first[chunk]
+        arrived(g, kv, FAR[blk])
 
         @pl.when(passes_down)
         def _():
@@ -182,24 +204,33 @@
         def _():
             up_copy(g, kv, blk).start()
 
-    def pass_up(g, blk):
-        arrived(g, 0, 4 + blk)
-        relay_up(g, blk).start()
+    def pass_up(g, blk, late):
+        @pl.when((y == 0) if late else (y > 0))
+        def _():
+            arrived(g, 0, NEXT[blk])
+            relay_up(g, blk).start()
 
     def pass_down(g, blk):
-        arrived(g, 1, 6 + blk)
+        arrived(g, 1, THIRD[blk])
         relay_down(g, blk).start()
 
+    send_far(0)
+    send_far(1)
     for g in range(2):
         for blk in range(2):
             for copy in local_tree(g, blk):
                 copy.wait()
     send_own(0)
 
+    for copy in small:
+        copy.wait()
+
+    order = [1 - head // 2, head // 2]
+
     ids = {slot: lax.rem(node * BLK_DEV + nodes * BLK_DEV - back, nodes * BLK_DEV) for slot, back in BACK.items()}
     depths = []
     for b in range(BR_DEV):
-        current = leaf[b]
+        current = leaf[order[b]]
         depth = jnp.int32(0)
         hits = {slot: jnp.int32(0) for slot in ids}
         for step in range(SUB):
@@ -228,7 +259,7 @@
         def rotate(field):
             return field * cosine + pltpu.roll(field, HD // 2, 1) * sine
 
-        rows = pl.ds(b * BQ, BQ)
+        rows = pl.ds(pl.multiple_of(order[b] * BQ, BQ), BQ)
         for g in range(2):
             for h in range(GROUP):
                 field = raw[rows, (g * GROUP + h) * HD : (g * GROUP + h + 1) * HD].astype(jnp.float32)
@@ -255,7 +286,7 @@
     for g in range(2):
         for b in range(BR_DEV):
             keys = own_keys[g, b]
-            values = with_ones(own[1, b * BQ : (b + 1) * BQ, g * HD : (g + 1) * HD])
+            values = with_ones(own[1, pl.ds(pl.multiple_of(order[b] * BQ, BQ), BQ), g * HD : (g + 1) * HD])
             for r in range(0, COLS, TILE):
                 scores = scores_of(keys, g, b, r)
                 key_at = lax.broadcasted_iota(jnp.int32, (BQ, TILE), 0)
@@ -268,9 +299,8 @@
                 totals[g, b, 0:1, r : r + TILE] = mixed[HD : HD + 1]
                 acc[g, b, :, r : r + TILE] = mixed[:HD]
 
-    tiles = [(b, r) for b in range(BR_DEV) for r in range(0, COLS, TILE)]
-
-    def attend(g, slot):
+    def attend(g, slot, branches=range(BR_DEV)):
+        tiles = [(b, r) for b in branches for r in range(0, COLS, TILE)]
         keys = kbuf[g, slot]
         values = with_ones(vbuf[g, slot])
         on = [live[b, slot] > 0 for b in range(BR_DEV)]
@@ -300,157 +330,110 @@
         for item in waiting:
             add(*item)
 
-    def finish(g):
-        for b in range(BR_DEV):
-            for h in range(GROUP):
-                span = slice(h * BQ, (h + 1) * BQ)
-                mixed = acc[g, b, :, span] / totals[g, b, 0:1, span]
-                obuf[b * BQ : (b + 1) * BQ, (g * GROUP + h) * HD : (g * GROUP + h + 1) * HD] = mixed.T.astype(
-                    jnp.bfloat16
-                )
+    def finish(g, b):
+        for h in range(GROUP):
+            span = slice(h * BQ, (h + 1) * BQ)
+            mixed = acc[g, b, :, span] / totals[g, b, 0:1, span]
+            obuf[b * BQ : (b + 1) * BQ, (g * GROUP + h) * HD : (g * GROUP + h + 1) * HD] = mixed.T.astype(
+                jnp.bfloat16
+            )
 
     part = BR_DEV * BQ // heads
 
-    def out_copy(g, k):
-        device = others[k - 1]
+    def out_copy(g, b, j):
+        device = order[b] * 2 + j
+        at = lax.rem(device - head + heads, heads) - 1
         return pltpu.make_async_remote_copy(
-            src_ref=obuf.at[pl.ds(pl.multiple_of(device * part, part), part), pl.ds(g * COLS, COLS)],
+            src_ref=obuf.at[pl.ds(b * BQ + j * part, part), pl.ds(g * COLS, COLS)],
             dst_ref=out.at[:, pl.ds(pl.multiple_of((head * 2 + g) * COLS, COLS), COLS)],
-            send_sem=out_send.at[g, k - 1],
-            recv_sem=out_recv.at[g, k - 1],
+            send_sem=out_send.at[g, at],
+            recv_sem=out_recv.at[g, at],
             device_id=(node, device),
             device_id_type=MESH,
         )
 
+    core = lax.rem(head, 2)
+
     def out_keep(g):
         return pltpu.make_async_copy(
-            obuf.at[pl.ds(pl.multiple_of(head * part, part), part), pl.ds(g * COLS, COLS)],
+            obuf.at[pl.ds(pl.multiple_of(BQ + core * part, part), part), pl.ds(g * COLS, COLS)],
             out.at[:, pl.ds(pl.multiple_of((head * 2 + g) * COLS, COLS), COLS)],
             out_local.at[g],
         )
 
-    def exchange(g):
-        for k in (2, 1, 3):
-            out_copy(g, k).start()
-        out_keep(g).start()
+    def exchange(g, b):
+        if b == 0:
+            for j in range(2):
+                out_copy(g, 0, j).start()
+        else:
+            out_copy(g, 1, 1 - core).start()
+            out_keep(g).start()
 
     for g in range(2):
         for copy in local_shared(g):
             copy.wait()
 
-    def local_step(i, carry):
-        attend(i // 3, lax.rem(i, 3))
-
-        @pl.when(i == 0)
+    def at(i, step, *services):
+        @pl.when(i == step)
         def _():
-            forward(0, 0)
-
-        @pl.when(i == 1)
-        def _():
-            forward(0, 1)
-            pass_up(0, 1)
-
-        @pl.when(i == 2)
-        def _():
-            pass_down(0, 1)
-
-        @pl.when(i == 3)
-        def _():
-            forward(0, 2)
-            send_own(1)
-
-        @pl.when(i == 4)
-        def _():
-            forward(0, 3)
-            pass_up(0, 0)
-
-        @pl.when(i == 5)
-        def _():
-            pass_down(0, 0)
-
+            for service in services:
+                service()
+
+    def first_step(i, carry):
+        local = i < 6
+        g = jnp.where(local, i // 3, 0)
+        slot = jnp.where(local, lax.rem(i, 3), i - 6 + FIRST)
+        at(i, 1, lambda: forward(0, 0), lambda: pass_up(0, 1, False))
+        at(i, 3, lambda: forward(0, 1), lambda: pass_up(0, 0, False))
+        at(i, 4, lambda: pass_down(0, 1))
+        at(i, 5, lambda: forward(0, 2))
+        at(i, 6, lambda: pass_down(0, 0))
+        at(i, 7, lambda: forward(0, 3), lambda: pass_up(0, 1, True), lambda: arrived(0, 1, NEXT[1]))
+        at(i, 8, lambda: forward(1, 0), lambda: pass_up(0, 0, True), lambda: arrived(0, 1, NEXT[0]))
+        at(i, 9, lambda: send_own(1), lambda: arrived(0, 0, THIRD[1]))
+        at(i, 10, lambda: forward(1, 1), lambda: arrived(0, 0, SECOND[1]), lambda: arrived(0, 1, SECOND[1]))
+        at(i, 11, lambda: arrived(0, 0, SECOND[0]), lambda: arrived(0, 1, SECOND[0]))
+        at(i, 12, lambda: forward(1, 2), lambda: arrived(0, 0, THIRD[0]))
+        attend(g, slot)
         return carry
 
-    lax.fori_loop(0, 6, local_step, 0)
-
-    def first_step(i, carry):
-        slot = FIRST + i
-
-        @pl.when((i == 1) | (i == 2))
-        def _():
-            arrived(0, 1, slot)
-
-        @pl.when((i == 3) | (i == 4))
-        def _():
-            arrived(0, 0, slot)
-
-        @pl.when(i >= 5)
-        def _():
-            arrived(0, 0, slot)
-            arrived(0, 1, slot)
-
-        @pl.when(i == 2)
-        def _():
-            forward(1, 0)
-
-        @pl.when(i == 3)
-        def _():
-            forward(1, 1)
-            pass_up(1, 1)
-
-        @pl.when(i == 4)
-        def _():
-            pass_down(1, 1)
-
-        @pl.when(i == 5)
-        def _():
-            forward(1, 2)
-
-        @pl.when(i == 6)
-        def _():
-            forward(1, 3)
-
-        attend(0, slot)
-        return carry
-
-    lax.fori_loop(0, REMOTE, first_step, 0)
-    pass_up(1, 0)
-    pass_down(1, 0)
-    finish(0)
-    exchange(0)
+    lax.fori_loop(0, 6 + REMOTE, first_step, 0)
+    forward(1, 3)
+    pass_up(1, 1, False)
+    for b in range(BR_DEV):
+        finish(0, b)
+        exchange(0, b)
 
     def second_step(i, carry):
-        slot = FIRST + i
-
-        @pl.when((i == 1) | (i == 2))
-        def _():
-            arrived(1, 1, slot)
-
-        @pl.when((i == 3) | (i == 4))
-        def _():
-            arrived(1, 0, slot)
-
-        @pl.when(i >= 5)
-        def _():
-            arrived(1, 0, slot)
-            arrived(1, 1, slot)
-
+        slot = jnp.where(i < 4, FIRST + i, jnp.where(i == 4, THIRD[0], FIRST + i - 1))
+        at(i, 0, lambda: pass_up(1, 0, False), lambda: pass_down(1, 1))
+        at(i, 1, lambda: pass_down(1, 0), lambda: pass_up(1, 1, True), lambda: arrived(1, 1, NEXT[1]))
+        at(i, 2, lambda: pass_up(1, 0, True), lambda: arrived(1, 1, NEXT[0]))
+        at(i, 3, lambda: arrived(1, 0, THIRD[1]))
+        at(i, 4, lambda: arrived(1, 0, THIRD[0]))
+        at(i, 5, lambda: arrived(1, 0, SECOND[1]), lambda: arrived(1, 1, SECOND[1]))
         attend(1, slot)
         return carry
 
-    lax.fori_loop(0, REMOTE, second_step, 0)
-    finish(1)
-    exchange(1)
+    lax.fori_loop(0, REMOTE - 1, second_step, 0)
+    arrived(1, 0, SECOND[0])
+    arrived(1, 1, SECOND[0])
+    for b in range(BR_DEV):
+        attend(1, SECOND[0], (b,))
+        finish(1, b)
+        exchange(1, b)
 
     for g in range(2):
-        for kv, blk in chunks:
+        for kv, blk in values_first:
             z_copy(g, kv, blk).wait_send()
             up_copy(g, kv, blk).wait_send()
             down_copy(g, kv, blk).wait_send()
         for blk in range(2):
             relay_up(g, blk).wait_send()
             relay_down(g, blk).wait_send()
-        for k in range(1, heads):
-            out_copy(g, k).wait()
+        for j in range(2):
+            out_copy(g, 0, j).wait()
+        out_copy(g, 1, 1 - core).wait()
         out_keep(g).wait()
 
 
@@ -466,7 +449,6 @@
     rows = queries.shape[0]
     dma = pltpu.SemaphoreType.DMA
     anywhere = pl.BlockSpec(memory_space=pl.ANY)
-    scalars = pl.BlockSpec(memory_space=pltpu.SMEM)
 
     def kernel(*refs):
         attention_kernel(nodes, *refs)
@@ -474,15 +456,7 @@
     return pl.pallas_call(
         kernel,
         out_shape=jax.ShapeDtypeStruct((rows // heads, queries.shape[1] * heads), jnp.bfloat16),
-        in_specs=[
-            scalars,
-            scalars,
-            pl.BlockSpec(memory_space=pltpu.VMEM),
-            anywhere,
-            anywhere,
-            anywhere,
-            anywhere,
-        ],
+        in_specs=[anywhere] * 7,
         out_specs=anywhere,
         scratch_shapes=[
             pltpu.VMEM(queries.shape, jnp.bfloat16),
@@ -495,7 +469,11 @@
             pltpu.VMEM((2, BR_DEV, 8, COLS), jnp.float32),
             pltpu.VMEM((2, BR_DEV, HD, COLS), jnp.float32),
             pltpu.VMEM(queries.shape, jnp.bfloat16),
+            pltpu.SMEM(parent.shape, jnp.int32),
+            pltpu.SMEM(leaf.shape, jnp.int32),
+            pltpu.VMEM((1, HD), jnp.float32),
             pltpu.SMEM((BR_DEV, 16), jnp.int32),
+            dma((3,)),
             dma,
             dma,
             dma((2, 3)),
@@ -512,7 +490,7 @@
             dma((2,)),
         ],
         compiler_params=pltpu.CompilerParams(
-            collective_id=0, has_side_effects=True, vmem_limit_bytes=48 * 1024 * 1024
+            collective_id=0, has_side_effects=True, vmem_limit_bytes=64 * 1024 * 1024 - 64 * 1024
         ),
         name="branch_attention",
     )(parent, leaf, jnp.asarray(inverse_frequencies()), queries, own_cache, tree_cache, shared_cache)

time: 78.1 us -> 69.2 us (0.89)
  local copies, waits for them, and re-layouts: 7.38 us -> 2.26 us
  Pallas kernels: 70.4 us -> 66.8 us
    unnamed x15 -> x1, local copies, waits for them, and re-layouts: 7.38 us -> 2.26 us
    pallas_call x1, Pallas kernels: 70.4 us -> 66.8 us  [per_device(): pl.pallas_call(kernel, out_shape=jax.ShapeDtypeStruct((rows // heads, que...]
where the time goes in v2:
time: 69.2 us; the launch traced here: 69.1 us
  Pallas kernels  66.8 us (97%)
  local copies, waits for them, and re-layouts  2.26 us (3%)
    pallas_call x1, Pallas kernels, per_device(): pl.pallas_call(kernel, out_shape=jax.ShapeDtypeStruct((rows // heads, que...  66.8 us
    unnamed x1, local copies, waits for them, and re-layouts  2.26 us

profile of v2, /device:TPU:1, one launch (start us, length us, event | category | flops | bytes accessed | tf_op | source)
XLA Modules:
  0.0 69.1 jit_solution(13826853383530855440)
XLA Ops:
  0.0 66.8 %branch_attention.1 = bf16[64,8192]{1,0:T(8,128)(2,1)} custom-call(s32[128]{0:T(128)} %refs_0_.1, s32[2]{0:T(128)} %refs_1_.1, f32[1,128]{1,0:T(1,128)} %constant.2.clone.refs_2_, bf16[256,2048]{1,0:T(8,128)(2,1)} %refs_3_.1, bf16[2,256,256]{2,1,0:T(8,128)(2,1)} %refs_4_.1, bf16[2,1024,256]{2,1,0:T(8,128)(2,1)} %refs_5_.1, bf16[2,512,256]{2,1,0:T(8,128)(2,1)} %refs_6_.1), custom_call_target="tpu_custom_call" | custom-call | tf_op jit(solution)/shard_map/branch_attention/pallas_call | solution.py:456
  66.8 2.3 %copy.9 = bf16[64,8192]{1,0:T(8,128)(2,1)} copy(bf16[64,8192]{1,0:T(8,128)(2,1)} %branch_attention.1) | data formatting | bytes 2097152

commit v3 on v2

--- a/solution.py
+++ b/solution.py
@@ -21,6 +21,7 @@
 AHEAD = 2
 LAG = 1
 ONES = 16
+PIECES = 1
 
 BASE = 1000000.0
 NEG = -1e30
@@ -35,6 +36,121 @@
 FIRST = 3
 REMOTE = 7
 BACK = {0: 0, 1: -1, 3: 7, 4: 1, 5: 2, 6: 5, 9: 6, 7: 3, 8: 4}
+
+PLAN = {
+    0: (
+        (0, (("far", 1, 1, 1),)),
+        (1, (("up", 0, 1, 0), ("down", 0, 1, 1), ("up", 1, 1, 0), ("far", 0, 0, 1),)),
+        (3, (("up", 0, 0, 0),)),
+        (4, (("down", 0, 0, 0), ("up", 0, 1, 1),)),
+        (5, (("up", 0, 0, 1), ("down", 0, 0, 1),)),
+        (6, (("values", 0, 1), ("down", 0, 1, 0), ("up", 1, 1, 1),)),
+        (7, (("up", 1, 0, 0),)),
+        (8, (("far", 0, 1, 1), ("down", 1, 0, 1),)),
+        (10, (("far", 1, 0, 1),)),
+        (11, (("down", 1, 1, 0),)),
+        (12, (("down", 1, 1, 1),)),
+        (13, (("down", 1, 0, 0),)),
+        (14, (("up", 1, 0, 1), ("keys", 0, 1),)),
+        (15, (("values", 1, 1),)),
+        (19, (("values", 0, 0),)),
+        (20, (("keys", 1, 0), ("values", 1, 0), ("keys", 1, 1),)),
+        (21, (("keys", 0, 0),)),
+    ),
+    1: (
+        (0, (("far", 0, 1, 0), ("far", 0, 1, 1),)),
+        (1, (("up", 0, 0, 0), ("far", 0, 0, 1), ("up", 0, 1, 0),)),
+        (2, (("far", 0, 0, 0), ("on", 0, 1, 0), ("far", 1, 1, 0), ("far", 1, 1, 1),)),
+        (3, (("up", 0, 0, 1), ("on", 0, 1, 1),)),
+        (4, (("up", 0, 1, 1), ("keys", 0, 0),)),
+        (5, (("far", 1, 0, 0), ("values", 0, 0), ("up", 1, 1, 1),)),
+        (7, (("on", 0, 0, 1), ("on", 0, 0, 0),)),
+        (8, (("far", 1, 0, 1),)),
+        (11, (("on", 1, 1, 0), ("up", 1, 1, 0), ("up", 1, 0, 0),)),
+        (12, (("up", 1, 0, 1), ("on", 1, 1, 1),)),
+        (14, (("on", 1, 0, 0),)),
+        (16, (("keys", 1, 1), ("values", 1, 1),)),
+        (17, (("keys", 1, 0),)),
+        (18, (("keys", 0, 1),)),
+        (20, (("values", 1, 0),)),
+        (21, (("on", 1, 0, 1), ("values", 0, 1),)),
+    ),
+    3: (
+        (0, (("far", 0, 1, 0), ("far", 0, 1, 1),)),
+        (2, (("far", 0, 0, 1), ("on", 0, 1, 0),)),
+        (3, (("keys", 0, 0), ("far", 0, 0, 0), ("values", 0, 1),)),
+        (4, (("on", 0, 1, 1),)),
+        (6, (("far", 1, 1, 1),)),
+        (7, (("on", 0, 0, 1), ("far", 1, 1, 0),)),
+        (9, (("on", 0, 0, 0), ("far", 1, 0, 1),)),
+        (10, (("far", 1, 0, 0),)),
+        (11, (("on", 1, 1, 1),)),
+        (12, (("values", 0, 0),)),
+        (14, (("on", 1, 1, 0),)),
+        (16, (("on", 1, 0, 0),)),
+        (17, (("keys", 0, 1), ("values", 1, 1), ("keys", 1, 0),)),
+        (18, (("values", 1, 0),)),
+        (20, (("keys", 1, 1),)),
+        (21, (("on", 1, 0, 1),)),
+    ),
+}
+FIRST_ORDER = (4, 6, 9, 5, 3, 7, 8)
+SECOND_ORDER = (3, 4, 9, 6, 5, 7, 8)
+
+
+def planned_steps(place, blocks):
+    waited, sent = set(), set()
+    steps = [[] for _ in range(len(blocks) + 2)]
+
+    def wait(actions, *key):
+        if key not in waited:
+            waited.add(key)
+            actions.append(("wait",) + key)
+
+    def send(actions, op, g, *rest):
+        if (op, g) + rest in sent:
+            return
+        if op == "values" and not any(other[0] == "values" for other in sent):
+            actions.append(("ready", g))
+        sent.add((op, g) + rest)
+        for piece in range(PIECES):
+            if op == "on":
+                kv, blk = rest
+                wait(actions, g, kv, FAR[blk], piece)
+                actions.append(("down", g, kv, blk, piece))
+                if place == 3:
+                    actions.append(("up", g, kv, blk, piece))
+            else:
+                if op == "keys":
+                    wait(actions, g, 0, NEXT[rest[0]], piece)
+                elif op == "values":
+                    wait(actions, g, 1, THIRD[rest[0]], piece)
+                actions.append((op, g) + rest + (piece,))
+
+    early = {step: ops for step, ops in PLAN[place]}
+    for step, actions in enumerate(steps):
+        for op in early.get(step, ()):
+            send(actions, *op)
+        if step < 2:
+            continue
+        if step == len(steps) - 1:
+            for ops in early.values():
+                for op in ops:
+                    send(actions, *op)
+        g, slot = blocks[step - 2]
+        for blk in range(2):
+            if slot == FAR[blk] and place != 0:
+                send(actions, "on", g, 0, blk)
+                send(actions, "on", g, 1, blk)
+            if slot == NEXT[blk]:
+                send(actions, "keys", g, blk)
+            if slot == THIRD[blk]:
+                send(actions, "values", g, blk)
+        if slot >= FIRST:
+            for kv in range(2):
+                for piece in range(PIECES):
+                    wait(actions, g, kv, slot, piece)
+    return steps
 
 
 def attention_kernel(
@@ -62,6 +178,7 @@
     inverse,
     live,
     small_sem,
+    ready_sem,
     load_sem,
     own_sem,
     local_k,
@@ -90,6 +207,12 @@
     behind = lax.rem(node + nodes - RING, nodes)
     others = [lax.rem(head + k, heads) for k in range(1, heads)]
 
+    barrier = pltpu.get_barrier_semaphore()
+    for source in (down, up, behind, before):
+        pl.semaphore_signal(barrier, inc=1, device_id=(source, head), device_id_type=MESH)
+    for other in others:
+        pl.semaphore_signal(barrier, inc=1, device_id=(node, other), device_id_type=MESH)
+
     def local_tree(g, blk):
         rows = pl.ds(blk * BT, BT)
         columns = pl.ds(g * HD, HD)
@@ -124,22 +247,21 @@
         for copy in local_shared(g):
             copy.start()
 
-    barrier = pltpu.get_barrier_semaphore()
-    for source in (down, up, behind, before, after):
-        pl.semaphore_signal(barrier, inc=1, device_id=(source, head), device_id_type=MESH)
-    for other in others:
-        pl.semaphore_signal(barrier, inc=1, device_id=(node, other), device_id_type=MESH)
-    pl.semaphore_wait(barrier, 8)
+    pl.semaphore_wait(barrier, 7)
+    pl.semaphore_signal(ready_sem, inc=1, device_id=(after, head), device_id_type=MESH)
 
     bufs = (kbuf, vbuf)
     recvs = (recv_k, recv_v)
 
-    def remote(kv, g, source, target, sem, device):
+    def rows_of(piece):
+        return pl.ds(piece * (BT // PIECES), BT // PIECES)
+
+    def remote(kv, g, source, target, piece, sem, device):
         return pltpu.make_async_remote_copy(
-            src_ref=bufs[kv].at[g, source],
-            dst_ref=bufs[kv].at[g, target],
+            src_ref=bufs[kv].at[g, source, rows_of(piece)],
+            dst_ref=bufs[kv].at[g, target, rows_of(piece)],
             send_sem=sem,
-            recv_sem=recvs[kv].at[g, target],
+            recv_sem=recvs[kv].at[g, target, piece],
             device_id=(device, head),
             device_id_type=MESH,
         )
@@ -147,80 +269,71 @@
     passes_up = y == RING - 1
     passes_down = y > 0
 
-    def z_copy(g, kv, blk):
+    def z_copy(g, kv, blk, piece):
+        rows = pl.ds(blk * BT + piece * (BT // PIECES), BT // PIECES)
         return pltpu.make_async_remote_copy(
-            src_ref=tree_cache.at[kv, pl.ds(blk * BT, BT), pl.ds(g * HD, HD)],
-            dst_ref=bufs[kv].at[g, FAR[blk]],
-            send_sem=z_send.at[g, kv, blk],
-            recv_sem=recvs[kv].at[g, FAR[blk]],
+            src_ref=tree_cache.at[kv, rows, pl.ds(g * HD, HD)],
+            dst_ref=bufs[kv].at[g, FAR[blk], rows_of(piece)],
+            send_sem=z_send.at[g, kv, blk, piece],
+            recv_sem=recvs[kv].at[g, FAR[blk], piece],
             device_id=(ahead, head),
             device_id_type=MESH,
         )
 
-    def up_copy(g, kv, blk):
+    def up_copy(g, kv, blk, piece):
         source = jnp.where(passes_up, FAR[blk], blk)
-        return remote(kv, g, source, NEXT[blk], up_send.at[g, kv, blk], up)
-
-    def down_copy(g, kv, blk):
+        return remote(kv, g, source, NEXT[blk], piece, up_send.at[g, kv, blk, piece], up)
+
+    def down_copy(g, kv, blk, piece):
         source = jnp.where(passes_down, FAR[blk], blk)
-        return remote(kv, g, source, THIRD[blk], down_send.at[g, kv, blk], down)
-
-    def relay_up(g, blk):
-        return remote(0, g, NEXT[blk], SECOND[blk], relay_up_send.at[g, blk], after)
-
-    def relay_down(g, blk):
-        return remote(1, g, THIRD[blk], SECOND[blk], relay_down_send.at[g, blk], before)
-
-    def arrived(g, kv, slot):
-        pltpu.make_async_copy(bufs[kv].at[g, slot], bufs[kv].at[g, slot], recvs[kv].at[g, slot]).wait()
-
-    values_first = ((1, 1), (1, 0), (0, 1), (0, 0))
-    keys_first = ((0, 1), (0, 0), (1, 1), (1, 0))
-
-    def send_far(g):
-        for kv, blk in values_first:
-            z_copy(g, kv, blk).start()
-
-    def send_own(g):
-        @pl.when(jnp.logical_not(passes_up))
-        def _():
-            for kv, blk in keys_first:
-                up_copy(g, kv, blk).start()
-
-        @pl.when(jnp.logical_not(passes_down))
-        def _():
-            for kv, blk in values_first:
-                down_copy(g, kv, blk).start()
-
-    def forward(g, chunk):
-        kv, blk = values_first[chunk]
-        arrived(g, kv, FAR[blk])
-
-        @pl.when(passes_down)
-        def _():
-            down_copy(g, kv, blk).start()
-
-        @pl.when(passes_up)
-        def _():
-            up_copy(g, kv, blk).start()
-
-    def pass_up(g, blk, late):
-        @pl.when((y == 0) if late else (y > 0))
-        def _():
-            arrived(g, 0, NEXT[blk])
-            relay_up(g, blk).start()
-
-    def pass_down(g, blk):
-        arrived(g, 1, THIRD[blk])
-        relay_down(g, blk).start()
-
-    send_far(0)
-    send_far(1)
+        return remote(kv, g, source, THIRD[blk], piece, down_send.at[g, kv, blk, piece], down)
+
+    def relay_up(g, blk, piece):
+        return remote(0, g, NEXT[blk], SECOND[blk], piece, relay_up_send.at[g, blk, piece], after)
+
+    def relay_down(g, blk, piece):
+        return remote(1, g, THIRD[blk], SECOND[blk], piece, relay_down_send.at[g, blk, piece], before)
+
+    def arrived(g, kv, slot, piece):
+        here = bufs[kv].at[g, slot, rows_of(piece)]
+        pltpu.make_async_copy(here, here, recvs[kv].at[g, slot, piece]).wait()
+
+    def act(op, g, *rest):
+        if op == "wait":
+            arrived(g, *rest)
+        elif op == "far":
+            z_copy(g, *rest).start()
+        elif op == "up":
+            up_copy(g, *rest).start()
+        elif op == "down":
+            down_copy(g, *rest).start()
+        elif op == "keys":
+            relay_up(g, *rest).start()
+        elif op == "values":
+            relay_down(g, *rest).start()
+        else:
+            pl.semaphore_wait(ready_sem, 1)
+
+    blocks = [(g, slot) for g in range(2) for slot in range(3)]
+    blocks += [(0, slot) for slot in FIRST_ORDER] + [(1, slot) for slot in SECOND_ORDER]
+    plans = {place: planned_steps(place, blocks) for place in PLAN}
+    at_place = {0: y == 0, 1: (y == 1) | (y == 2), 3: y == 3}
+
+    def serve(step):
+        for place, plan in plans.items():
+            if plan[step]:
+
+                @pl.when(at_place[place])
+                def _():
+                    for action in plan[step]:
+                        act(*action)
+
+    serve(0)
     for g in range(2):
         for blk in range(2):
             for copy in local_tree(g, blk):
                 copy.wait()
-    send_own(0)
+    serve(1)
 
     for copy in small:
         copy.wait()
@@ -373,64 +486,61 @@
         for copy in local_shared(g):
             copy.wait()
 
-    def at(i, step, *services):
-        @pl.when(i == step)
-        def _():
-            for service in services:
-                service()
+    def serve_at(i, steps):
+        for step in steps:
+            if any(plan[step + 2] for plan in plans.values()):
+
+                @pl.when(i == step)
+                def _():
+                    serve(step + 2)
+
+    def pick(i, values):
+        result = jnp.int32(values[0])
+        for at, value in enumerate(values[1:]):
+            result = jnp.where(i == at + 1, value, result)
+        return result
+
+    first = 6 + REMOTE
 
     def first_step(i, carry):
-        local = i < 6
-        g = jnp.where(local, i // 3, 0)
-        slot = jnp.where(local, lax.rem(i, 3), i - 6 + FIRST)
-        at(i, 1, lambda: forward(0, 0), lambda: pass_up(0, 1, False))
-        at(i, 3, lambda: forward(0, 1), lambda: pass_up(0, 0, False))
-        at(i, 4, lambda: pass_down(0, 1))
-        at(i, 5, lambda: forward(0, 2))
-        at(i, 6, lambda: pass_down(0, 0))
-        at(i, 7, lambda: forward(0, 3), lambda: pass_up(0, 1, True), lambda: arrived(0, 1, NEXT[1]))
-        at(i, 8, lambda: forward(1, 0), lambda: pass_up(0, 0, True), lambda: arrived(0, 1, NEXT[0]))
-        at(i, 9, lambda: send_own(1), lambda: arrived(0, 0, THIRD[1]))
-        at(i, 10, lambda: forward(1, 1), lambda: arrived(0, 0, SECOND[1]), lambda: arrived(0, 1, SECOND[1]))
-        at(i, 11, lambda: arrived(0, 0, SECOND[0]), lambda: arrived(0, 1, SECOND[0]))
-        at(i, 12, lambda: forward(1, 2), lambda: arrived(0, 0, THIRD[0]))
-        attend(g, slot)
+        serve_at(i, range(first))
+        attend(pick(i, [g for g, _ in blocks[:first]]), pick(i, [slot for _, slot in blocks[:first]]))
         return carry
 
-    lax.fori_loop(0, 6 + REMOTE, first_step, 0)
-    forward(1, 3)
-    pass_up(1, 1, False)
+    lax.fori_loop(0, first, first_step, 0)
     for b in range(BR_DEV):
         finish(0, b)
         exchange(0, b)
 
+    last = len(blocks) - 1
+
     def second_step(i, carry):
-        slot = jnp.where(i < 4, FIRST + i, jnp.where(i == 4, THIRD[0], FIRST + i - 1))
-        at(i, 0, lambda: pass_up(1, 0, False), lambda: pass_down(1, 1))
-        at(i, 1, lambda: pass_down(1, 0), lambda: pass_up(1, 1, True), lambda: arrived(1, 1, NEXT[1]))
-        at(i, 2, lambda: pass_up(1, 0, True), lambda: arrived(1, 1, NEXT[0]))
-        at(i, 3, lambda: arrived(1, 0, THIRD[1]))
-        at(i, 4, lambda: arrived(1, 0, THIRD[0]))
-        at(i, 5, lambda: arrived(1, 0, SECOND[1]), lambda: arrived(1, 1, SECOND[1]))
-        attend(1, slot)
+        serve_at(i + first, range(first, last))
+        attend(1, pick(i, SECOND_ORDER[:-1]))
         return carry
 
-    lax.fori_loop(0, REMOTE - 1, second_step, 0)
-    arrived(1, 0, SECOND[0])
-    arrived(1, 1, SECOND[0])
+    lax.fori_loop(0, last - first, second_step, 0)
+    serve(last + 2)
     for b in range(BR_DEV):
-        attend(1, SECOND[0], (b,))
+        attend(1, SECOND_ORDER[-1], (b,))
         finish(1, b)
         exchange(1, b)
 
     for g in range(2):
-        for kv, blk in values_first:
-            z_copy(g, kv, blk).wait_send()
-            up_copy(g, kv, blk).wait_send()
-            down_copy(g, kv, blk).wait_send()
-        for blk in range(2):
-            relay_up(g, blk).wait_send()
-            relay_down(g, blk).wait_send()
+        for piece in range(PIECES):
+            for blk in range(2):
+                for kv in range(2):
+                    up_copy(g, kv, blk, piece).wait_send()
+                    down_copy(g, kv, blk, piece).wait_send()
+                relay_up(g, blk, piece).wait_send()
+                relay_down(g, blk, piece).wait_send()
+            for kv in range(2):
+                z_copy(g, kv, 1, piece).wait_send()
+
+                @pl.when(y > 0)
+                def _():
+                    z_copy(g, kv, 0, piece).wait_send()
+
         for j in range(2):
             out_copy(g, 0, j).wait()
         out_copy(g, 1, 1 - core).wait()
@@ -474,17 +584,18 @@
             pltpu.VMEM((1, HD), jnp.float32),
             pltpu.SMEM((BR_DEV, 16), jnp.int32),
             dma((3,)),
+            pltpu.SemaphoreType.REGULAR,
             dma,
             dma,
             dma((2, 3)),
             dma((2, 3)),
-            dma((2, 2, 2)),
-            dma((2, 2, 2)),
-            dma((2, 2, 2)),
-            dma((2, 2)),
-            dma((2, 2)),
-            dma((2, SLOTS)),
-            dma((2, SLOTS)),
+            dma((2, 2, 2, PIECES)),
+            dma((2, 2, 2, PIECES)),
+            dma((2, 2, 2, PIECES)),
+            dma((2, 2, PIECES)),
+            dma((2, 2, PIECES)),
+            dma((2, SLOTS, PIECES)),
+            dma((2, SLOTS, PIECES)),
             dma((2, 3)),
             dma((2, 3)),
             dma((2,)),

time: 69.2 us -> 64.8 us (0.936)
  Pallas kernels: 66.8 us -> 62 us
    pallas_call x1, Pallas kernels: 66.8 us -> 62 us  [per_device(): pl.pallas_call(kernel, out_shape=jax.ShapeDtypeStruct((rows // heads, que...]
where the time goes in v3:
time: 64.8 us; the launch traced here: 64.2 us
  Pallas kernels  62 us (96%)
  local copies, waits for them, and re-layouts  2.26 us (3%)
    pallas_call x1, Pallas kernels, per_device(): pl.pallas_call(kernel, out_shape=jax.ShapeDtypeStruct((rows // heads, que...  62 us
    unnamed x1, local copies, waits for them, and re-layouts  2.26 us

profile of v3, /device:TPU:1, one launch (start us, length us, event | category | flops | bytes accessed | tf_op | source)
XLA Modules:
  0.0 64.2 jit_solution(667161789186000630)
XLA Ops:
  0.0 62.0 %branch_attention.1 = bf16[64,8192]{1,0:T(8,128)(2,1)} custom-call(s32[128]{0:T(128)} %refs_0_.1, s32[2]{0:T(128)} %refs_1_.1, f32[1,128]{1,0:T(1,128)} %constant.2.clone.refs_2_, bf16[256,2048]{1,0:T(8,128)(2,1)} %refs_3_.1, bf16[2,256,256]{2,1,0:T(8,128)(2,1)} %refs_4_.1, bf16[2,1024,256]{2,1,0:T(8,128)(2,1)} %refs_5_.1, bf16[2,512,256]{2,1,0:T(8,128)(2,1)} %refs_6_.1), custom_call_target="tpu_custom_call" | custom-call | tf_op jit(solution)/shard_map/branch_attention/pallas_call | solution.py:566
  62.0 2.3 %copy.9 = bf16[64,8192]{1,0:T(8,128)(2,1)} copy(bf16[64,8192]{1,0:T(8,128)(2,1)} %branch_attention.1) | data formatting | bytes 2097152

commit v4 on v3

--- a/solution.py
+++ b/solution.py
@@ -40,62 +40,59 @@
 PLAN = {
     0: (
         (0, (("far", 1, 1, 1),)),
-        (1, (("up", 0, 1, 0), ("down", 0, 1, 1), ("up", 1, 1, 0), ("far", 0, 0, 1),)),
-        (3, (("up", 0, 0, 0),)),
-        (4, (("down", 0, 0, 0), ("up", 0, 1, 1),)),
-        (5, (("up", 0, 0, 1), ("down", 0, 0, 1),)),
-        (6, (("values", 0, 1), ("down", 0, 1, 0), ("up", 1, 1, 1),)),
-        (7, (("up", 1, 0, 0),)),
-        (8, (("far", 0, 1, 1), ("down", 1, 0, 1),)),
-        (10, (("far", 1, 0, 1),)),
-        (11, (("down", 1, 1, 0),)),
-        (12, (("down", 1, 1, 1),)),
-        (13, (("down", 1, 0, 0),)),
-        (14, (("up", 1, 0, 1), ("keys", 0, 1),)),
-        (15, (("values", 1, 1),)),
-        (19, (("values", 0, 0),)),
-        (20, (("keys", 1, 0), ("values", 1, 0), ("keys", 1, 1),)),
-        (21, (("keys", 0, 0),)),
+        (1, (("up", 1, 1, 0), ("down", 0, 1, 1), ("down", 1, 0, 1), ("up", 0, 0, 1), ("up", 0, 1, 1),)),
+        (2, (("far", 1, 0, 1),)),
+        (3, (("down", 0, 0, 0), ("far", 0, 1, 1),)),
+        (4, (("up", 1, 0, 1), ("up", 0, 1, 0), ("up", 1, 0, 0),)),
+        (5, (("down", 0, 0, 1),)),
+        (6, (("far", 0, 0, 1), ("down", 0, 1, 0), ("up", 0, 0, 0),)),
+        (9, (("down", 1, 1, 0),)),
+        (11, (("down", 1, 1, 1),)),
+        (12, (("up", 1, 1, 1),)),
+        (13, (("values", 1, 1), ("down", 1, 0, 0), ("keys", 0, 0),)),
+        (14, (("values", 0, 1),)),
+        (15, (("values", 1, 0),)),
+        (17, (("keys", 1, 0), ("keys", 1, 1),)),
+        (18, (("values", 0, 0),)),
+        (19, (("keys", 0, 1),)),
     ),
     1: (
-        (0, (("far", 0, 1, 0), ("far", 0, 1, 1),)),
-        (1, (("up", 0, 0, 0), ("far", 0, 0, 1), ("up", 0, 1, 0),)),
-        (2, (("far", 0, 0, 0), ("on", 0, 1, 0), ("far", 1, 1, 0), ("far", 1, 1, 1),)),
-        (3, (("up", 0, 0, 1), ("on", 0, 1, 1),)),
-        (4, (("up", 0, 1, 1), ("keys", 0, 0),)),
-        (5, (("far", 1, 0, 0), ("values", 0, 0), ("up", 1, 1, 1),)),
-        (7, (("on", 0, 0, 1), ("on", 0, 0, 0),)),
-        (8, (("far", 1, 0, 1),)),
-        (11, (("on", 1, 1, 0), ("up", 1, 1, 0), ("up", 1, 0, 0),)),
-        (12, (("up", 1, 0, 1), ("on", 1, 1, 1),)),
-        (14, (("on", 1, 0, 0),)),
-        (16, (("keys", 1, 1), ("values", 1, 1),)),
-        (17, (("keys", 1, 0),)),
-        (18, (("keys", 0, 1),)),
-        (20, (("values", 1, 0),)),
-        (21, (("on", 1, 0, 1), ("values", 0, 1),)),
+        (0, (("far", 0, 1, 1), ("far", 0, 0, 0),)),
+        (1, (("up", 0, 0, 1), ("up", 1, 1, 0),)),
+        (3, (("far", 0, 1, 0), ("on", 0, 1, 1), ("up", 0, 1, 1),)),
+        (4, (("on", 0, 0, 0), ("up", 0, 0, 0), ("far", 0, 0, 1), ("far", 1, 1, 0),)),
+        (5, (("up", 0, 1, 0), ("on", 0, 1, 0),)),
+        (6, (("values", 0, 1),)),
+        (7, (("far", 1, 1, 1), ("far", 1, 0, 0), ("up", 1, 0, 1),)),
+        (9, (("far", 1, 0, 1),)),
+        (11, (("keys", 0, 1),)),
+        (12, (("on", 1, 1, 1), ("on", 1, 1, 0), ("keys", 1, 1),)),
+        (14, (("up", 1, 0, 0), ("on", 1, 0, 0), ("up", 1, 1, 1), ("values", 0, 0), ("on", 0, 0, 1),)),
+        (17, (("values", 1, 1),)),
+        (18, (("keys", 1, 0),)),
+        (19, (("values", 1, 0),)),
+        (20, (("on", 1, 0, 1), ("keys", 0, 0),)),
     ),
     3: (
-        (0, (("far", 0, 1, 0), ("far", 0, 1, 1),)),
-        (2, (("far", 0, 0, 1), ("on", 0, 1, 0),)),
-        (3, (("keys", 0, 0), ("far", 0, 0, 0), ("values", 0, 1),)),
-        (4, (("on", 0, 1, 1),)),
-        (6, (("far", 1, 1, 1),)),
-        (7, (("on", 0, 0, 1), ("far", 1, 1, 0),)),
-        (9, (("on", 0, 0, 0), ("far", 1, 0, 1),)),
-        (10, (("far", 1, 0, 0),)),
-        (11, (("on", 1, 1, 1),)),
-        (12, (("values", 0, 0),)),
-        (14, (("on", 1, 1, 0),)),
-        (16, (("on", 1, 0, 0),)),
-        (17, (("keys", 0, 1), ("values", 1, 1), ("keys", 1, 0),)),
-        (18, (("values", 1, 0),)),
-        (20, (("keys", 1, 1),)),
-        (21, (("on", 1, 0, 1),)),
+        (0, (("far", 0, 1, 1), ("far", 0, 0, 1),)),
+        (2, (("values", 0, 1), ("far", 0, 1, 0),)),
+        (3, (("on", 0, 1, 1),)),
+        (4, (("far", 0, 0, 0),)),
+        (5, (("on", 0, 0, 1), ("keys", 0, 1),)),
+        (6, (("far", 1, 0, 0),)),
+        (7, (("on", 0, 1, 0),)),
+        (9, (("far", 1, 1, 0),)),
+        (10, (("on", 0, 0, 0),)),
+        (12, (("far", 1, 0, 1), ("on", 1, 0, 0), ("far", 1, 1, 1), ("on", 1, 1, 0),)),
+        (14, (("on", 1, 0, 1), ("keys", 1, 1),)),
+        (16, (("values", 1, 1),)),
+        (18, (("values", 0, 0), ("on", 1, 1, 1),)),
+        (20, (("keys", 1, 0),)),
+        (21, (("keys", 0, 0), ("values", 1, 0),)),
     ),
 }
-FIRST_ORDER = (4, 6, 9, 5, 3, 7, 8)
-SECOND_ORDER = (3, 4, 9, 6, 5, 7, 8)
+FIRST_ORDER = (4, 3, 9, 5, 6, 8, 7)
+SECOND_ORDER = (3, 5, 9, 6, 4, 7, 8)
 
 
 def planned_steps(place, blocks):

time: 64.8 us -> 63.8 us (0.985)
  Pallas kernels: 62 us -> 60.6 us
    pallas_call x1, Pallas kernels: 62 us -> 60.6 us  [per_device(): pl.pallas_call(kernel, out_shape=jax.ShapeDtypeStruct((rows // heads, que...]
where the time goes in v4:
time: 63.8 us; the launch traced here: 62.8 us
  Pallas kernels  60.6 us (95%)
  local copies, waits for them, and re-layouts  2.26 us (4%)
    pallas_call x1, Pallas kernels, per_device(): pl.pallas_call(kernel, out_shape=jax.ShapeDtypeStruct((rows // heads, que...  60.6 us
    unnamed x1, local copies, waits for them, and re-layouts  2.26 us

profile of v4, /device:TPU:1, one launch (start us, length us, event | category | flops | bytes accessed | tf_op | source)
XLA Modules:
  0.0 62.8 jit_solution(3166083747933580065)
XLA Ops:
  0.0 60.6 %branch_attention.1 = bf16[64,8192]{1,0:T(8,128)(2,1)} custom-call(s32[128]{0:T(128)} %refs_0_.1, s32[2]{0:T(128)} %refs_1_.1, f32[1,128]{1,0:T(1,128)} %constant.2.clone.refs_2_, bf16[256,2048]{1,0:T(8,128)(2,1)} %refs_3_.1, bf16[2,256,256]{2,1,0:T(8,128)(2,1)} %refs_4_.1, bf16[2,1024,256]{2,1,0:T(8,128)(2,1)} %refs_5_.1, bf16[2,512,256]{2,1,0:T(8,128)(2,1)} %refs_6_.1), custom_call_target="tpu_custom_call" | custom-call | tf_op jit(solution)/shard_map/branch_attention/pallas_call | solution.py:563
  60.6 2.3 %copy.9 = bf16[64,8192]{1,0:T(8,128)(2,1)} copy(bf16[64,8192]{1,0:T(8,128)(2,1)} %branch_attention.1) | data formatting | bytes 2097152

commit v5 on v4

--- a/solution.py
+++ b/solution.py
@@ -505,6 +505,7 @@
         return carry
 
     lax.fori_loop(0, first, first_step, 0)
+    serve(first + 2)
     for b in range(BR_DEV):
         finish(0, b)
         exchange(0, b)
@@ -512,7 +513,7 @@
     last = len(blocks) - 1
 
     def second_step(i, carry):
-        serve_at(i + first, range(first, last))
+        serve_at(i + first, range(first + 1, last))
         attend(1, pick(i, SECOND_ORDER[:-1]))
         return carry
 

time: 63.8 us -> 63.8 us (level)
  no operation moved by 1% of the time
where the time goes in v5:
time: 63.8 us; the launch traced here: 62.8 us
  Pallas kernels  60.5 us (95%)
  local copies, waits for them, and re-layouts  2.26 us (4%)
    pallas_call x1, Pallas kernels, per_device(): pl.pallas_call(kernel, out_shape=jax.ShapeDtypeStruct((rows // heads, que...  60.5 us
    unnamed x1, local copies, waits for them, and re-layouts  2.26 us

profile of v5, /device:TPU:1, one launch (start us, length us, event | category | flops | bytes accessed | tf_op | source)
XLA Modules:
  0.0 62.8 jit_solution(7493397030249880433)
XLA Ops:
  0.0 60.5 %branch_attention.1 = bf16[64,8192]{1,0:T(8,128)(2,1)} custom-call(s32[128]{0:T(128)} %refs_0_.1, s32[2]{0:T(128)} %refs_1_.1, f32[1,128]{1,0:T(1,128)} %constant.2.clone.refs_2_, bf16[256,2048]{1,0:T(8,128)(2,1)} %refs_3_.1, bf16[2,256,256]{2,1,0:T(8,128)(2,1)} %refs_4_.1, bf16[2,1024,256]{2,1,0:T(8,128)(2,1)} %refs_5_.1, bf16[2,512,256]{2,1,0:T(8,128)(2,1)} %refs_6_.1), custom_call_target="tpu_custom_call" | custom-call | tf_op jit(solution)/shard_map/branch_attention/pallas_call | solution.py:564
  60.5 2.3 %copy.9 = bf16[64,8192]{1,0:T(8,128)(2,1)} copy(bf16[64,8192]{1,0:T(8,128)(2,1)} %branch_attention.1) | data formatting | bytes 2097152
